TPU v7x, 32 devices: a whole 2x2x4 slice. The times are simulated.
32 devices in a mesh: gx: 8 (over y, x, core), gy: 4 (over z).
Axes of the slice: x: 2, y: 2, z: 4, core: 2. Of those that a mesh axis runs over, the one named last changes fastest.
Arguments:
- held_head: float32 [4096, 8, 128], P(('gx', 'gy')), may hold values from -6 to -0.5
- held_head_old: float32 [4096, 8, 128], P(('gx', 'gy')), may hold values from -6 to -0.5
- material_ids: int32 [128, 64, 512], P(None, 'gx', 'gy'), may hold values from 0 to 15
- block_map: int32 [32, 32], replicated, may hold values from 0 to 31, as said below
- conductivity: float32 [3, 16], replicated, may hold values from 0.1 to 10
- vg_alpha: float32 [16], replicated, may hold values from 0.5 to 4
- vg_n: float32 [16], replicated, may hold values from 1.5 to 3
- capacity: float32 [16], replicated, may hold values from 0.1 to 0.45
Outputs:
- update: float32 [128, 64, 512], P(None, 'gx', 'gy')
Inputs may be any that keep to these rules, and one draw needn't show every extreme that they name: Every row and every column of block_map holds each brick number once.
All inputs are finite; a program needn't handle non-finite values.
Results may differ from a plain program's by a relative error of at most 0.0001.
Values sent between devices are 32-bit elements; how exact they have to be, the bound alone decides.
A program may use at most 128 MiB of HBM per device.

v0:
```python
import jax
import jax.numpy as jnp
from jax import lax
from jax.sharding import PartitionSpec as P

MATERIALS = 16
ITERS = 4


STORE = 4.0


def extended(cells, sides, width):
    for axis, dim in sides:
        count = lax.axis_size(axis)
        ends = count - 1
        head = lax.slice_in_dim(cells, 0, width, axis=dim)
        tail = lax.slice_in_dim(cells, cells.shape[dim] - width, cells.shape[dim], axis=dim)
        cells = jnp.concatenate(
            [
                lax.ppermute(tail, axis, [(i, (i + 1) % count) for i in range(ends)]),
                cells,
                lax.ppermute(head, axis, [((i + 1) % count, i) for i in range(ends)]),
            ],
            axis=dim,
        )
    return cells


def retention(level, alpha_cell, expo_cell):
    scaled = alpha_cell * -level
    power = jnp.exp(expo_cell * jnp.log(scaled))
    exponent = 1.0 - 1.0 / expo_cell
    inverse = 1.0 / (1.0 + power)
    saturation = jnp.exp(exponent * jnp.log(inverse))
    inner_term = -jnp.expm1(exponent * jnp.log1p(-inverse))
    relperm = jnp.sqrt(saturation) * inner_term * inner_term
    return (saturation, relperm)


def properties(material_ids, conductivity, vg_alpha, vg_n, capacity):
    blank = jnp.zeros(material_ids.shape, conductivity.dtype)
    fields = [blank, blank, blank, blank, blank, blank]
    for m in range(MATERIALS):
        match_cell = material_ids == m
        values = (
            conductivity[0, m],
            conductivity[1, m],
            conductivity[2, m],
            vg_alpha[m],
            vg_n[m],
            capacity[m],
        )
        fields = [jnp.where(match_cell, value, field) for value, field in zip(values, fields)]
    return fields


def pair_slices(padded, axis):
    lower_index = [slice(1, -1), slice(1, -1), slice(1, -1)]
    higher_index = [slice(1, -1), slice(1, -1), slice(1, -1)]
    lower_index[axis] = slice(0, -1)
    higher_index[axis] = slice(1, None)
    return (padded[tuple(lower_index)], padded[tuple(higher_index)])


def face_terms(pad_head, pad_rel, pad_cond, axis, rise):
    head_low, head_high = pair_slices(pad_head, axis)
    rel_low, rel_high = pair_slices(pad_rel, axis)
    cond_low, cond_high = pair_slices(pad_cond, axis)
    trans = 2.0 * cond_low * cond_high / (cond_low + cond_high)
    potential = head_high - head_low + rise
    along = trans * (0.5 * (rel_low + rel_high))
    slope = trans * potential * 0.5
    return (along, slope, along * potential)


def net_inflow(flux, axis):
    extent = flux.shape[axis]
    return lax.slice_in_dim(flux, 1, extent, axis=axis) - lax.slice_in_dim(
        flux, 0, extent - 1, axis=axis
    )


def least_squares(hess, beta):
    matrix_rows = [hess[i] for i in range(ITERS + 1)]
    target = [beta] + [jnp.zeros_like(beta) for i in range(ITERS)]
    for j in range(ITERS):
        first = matrix_rows[j][j]
        second = matrix_rows[j + 1][j]
        radius = jnp.sqrt(first * first + second * second)
        cosine = first / radius
        sine_value = second / radius
        row_top, row_next = (matrix_rows[j], matrix_rows[j + 1])
        matrix_rows[j] = cosine * row_top + sine_value * row_next
        matrix_rows[j + 1] = cosine * row_next - sine_value * row_top
        goal_top, goal_next = (target[j], target[j + 1])
        target[j] = cosine * goal_top + sine_value * goal_next
        target[j + 1] = cosine * goal_next - sine_value * goal_top
    coeffs = [None] * ITERS
    for j in reversed(range(ITERS)):
        running = target[j]
        for k in range(j + 1, ITERS):
            running = running - matrix_rows[j][k] * coeffs[k]
        coeffs[j] = running / matrix_rows[j][j]
    return coeffs


def global_length(field):
    return jnp.sqrt(lax.psum(jnp.sum(field * field), ("gx", "gy")))


def body(held_head, held_head_old, material_ids, block_map, conductivity, vg_alpha, vg_n, capacity):
    devices = lax.axis_size(("gx", "gy"))
    own_index = lax.axis_index(("gx", "gy"))
    layers = held_head.shape[0]
    slab_depth = layers // devices
    brick_shape = held_head.shape
    piece_shape = (devices, slab_depth) + tuple(held_head.shape[1:])
    numbers = jnp.arange(devices, dtype=jnp.int32)
    own_row = block_map[own_index]
    send_order = jnp.sum(
        jnp.where(own_row[None, :] == numbers[:, None], numbers[None, :], 0), axis=1
    )
    outgoing_head = jnp.take(held_head.reshape(piece_shape), send_order, axis=0)
    outgoing_old = jnp.take(held_head_old.reshape(piece_shape), send_order, axis=0)
    incoming_head, incoming_old = (
        lax.all_to_all(outgoing_head, ("gx", "gy"), split_axis=0, concat_axis=0, tiled=True),
        lax.all_to_all(outgoing_old, ("gx", "gy"), split_axis=0, concat_axis=0, tiled=True),
    )
    source_of = jnp.sum(jnp.where(block_map == own_index, numbers[:, None], 0), axis=0)
    head = jnp.take(incoming_head, source_of, axis=0).reshape(brick_shape)
    head_old = jnp.take(incoming_old, source_of, axis=0).reshape(brick_shape)
    cond_x, cond_y, cond_z, alpha_cell, expo_cell, cap_cell = properties(
        material_ids, conductivity, vg_alpha, vg_n, capacity
    )
    ones_field = jnp.ones_like(head)
    (saturation, relperm), (d_sat, d_rel) = jax.jvp(
        lambda level: retention(level, alpha_cell, expo_cell), (head,), (ones_field,)
    )
    stacked = jnp.stack([head, relperm, d_rel, cond_x, cond_y])
    rimmed = extended(stacked, (("gx", 2), ("gy", 3)), 1)
    old_sat = retention(head_old, alpha_cell, expo_cell)[0]
    padded = jnp.pad(rimmed, ((0, 0), (1, 1), (0, 0), (0, 0)))
    pad_head = padded[0]
    pad_rel = padded[1]
    pad_drel = padded[2]
    layout = [(1, padded[3], 0.0), (2, padded[4], 0.0), (0, jnp.pad(cond_z, 1), 1.0)]
    coefficients = []
    total_in = None
    for axis, pad_cond, rise in layout:
        along, slope, flux = face_terms(pad_head, pad_rel, pad_cond, axis, rise)
        coefficients.append((axis, along, slope))
        inflow = net_inflow(flux, axis)
        total_in = inflow if total_in is None else total_in + inflow
    newton_residual = STORE * cap_cell * (saturation - old_sat) - total_in
    diagonal = STORE * cap_cell * d_sat
    start = -newton_residual
    beta = global_length(start)
    basis = [start / beta]
    hess = jnp.zeros((ITERS + 1, ITERS), newton_residual.dtype)
    for j in range(ITERS):
        field = basis[j]
        rim_field = extended(field, (("gx", 1), ("gy", 2)), 1)
        pad_field = jnp.pad(rim_field, ((1, 1), (0, 0), (0, 0)))
        pad_weighted = pad_drel * pad_field
        total_change = None
        for apply_axis, apply_along, apply_slope in coefficients:
            field_low, field_high = pair_slices(pad_field, apply_axis)
            weight_low, weight_high = pair_slices(pad_weighted, apply_axis)
            change = apply_along * (field_high - field_low) + apply_slope * (
                weight_low + weight_high
            )
            apply_inflow = net_inflow(change, apply_axis)
            total_change = apply_inflow if total_change is None else total_change + apply_inflow
        image = diagonal * field - total_change
        local_products = jnp.stack([jnp.sum(image * vector) for vector in basis])
        summed = lax.psum(local_products, ("gx", "gy"))
        products = [summed[k] for k in range(j + 1)]
        for k in range(j + 1):
            image = image - products[k] * basis[k]
        norm_value = global_length(image)
        for k in range(j + 1):
            hess = hess.at[k, j].set(products[k])
        hess = hess.at[j + 1, j].set(norm_value)
        if j + 1 < ITERS:
            basis.append(image / norm_value)
    coeffs = least_squares(hess, beta)
    update = coeffs[0] * basis[0]
    for k in range(1, ITERS):
        update = update + coeffs[k] * basis[k]
    return update


def solution(mesh):
    return jax.shard_map(
        body,
        mesh=mesh,
        in_specs=(
            P(("gx", "gy"), None, None),
            P(("gx", "gy"), None, None),
            P(None, "gx", "gy"),
            P(),
            P(),
            P(),
            P(),
            P(),
        ),
        out_specs=P(None, "gx", "gy"),
        check_vma=False,
    )
```

profile of v0, /device:TPU:0, one launch (start us, length us, event | category | flops | bytes accessed | tf_op | source)
XLA Modules:
  0.0 735.3 jit_solution(11120605939722939615)
XLA Ops:
  4.5 7.3 all-to-all-start
  14.7 11.4 %all-to-all-done = f32[32,4,8,128]{3,2,1,0:T(8,128)S(1)} async-done(((f32[32,4,8,128]{3,2,1,0:T(8,128)}), f32[32,4,8,128]{3,2,1,0:T(8,128)S(1)}, u32[]{:S(2)}, u32[]{:S(2)}) %all-to-all-start) | async-done | bytes 524320 | tf_op jit(solution)/shard_map/all_to_all | solution.py:127
  26.2 4.1 all-to-all-start.1
  31.0 13.3 %select_select_fusion = (f32[128,8,128]{2,1,0:T(8,128)S(1)}, pred[128,8,128]{2,1,0:T(8,128)(4,1)S(1)}, pred[128,8,128]{2,1,0:T(8,128)(4,1)S(1)}, pred[128,8,128]...) fusion(f32[]{:T(128)} %bitcast.109, ...), kind=kLoop, calls=%fused_computation.214 | loop fusion | flops 4194304 | bytes 3145792 | tf_op jit(solution)/shard_map/jit(_where)/select_n | solution.py:54
  49.4 21.3 %multiply_multiply_fusion.3 = (f32[128,8,128]{2,1,0:T(8,128)S(1)}, f32[128,8,128]{2,1,0:T(8,128)S(1)}, f32[128,8,128]{2,1,0:T(8,128)S(1)}) fusion(f32[32,4,8,128]{3,2,1,0:T(8,128)S(1)} %get-tuple-element.238, pred[128,8,128]{2,1,0:T(8,128)(4,1)S(1)} %copy-done.72, pred[128,8,128]{2,1,0:T(8,128)(4,1)S(1)} %get-tuple-element.233, ...), kind=kLoop, calls=%fused_computation.219 | loop fusion | flops 6553600 | bytes 4194432 | tf_op jit(solution)/shard_map/jvp()/mul | solution.py:35
  72.7 10.7 %bitcast_dynamic-update-slice_fusion.1 = f32[5,128,8,128]{3,2,1,0:T(8,128)S(1)} fusion(f32[5,128,8,128]{3,2,1,0:T(8,128)S(1)} %bitcast_dynamic-update-slice_fusion.2, pred[128,8,128]{2,1,0:T(8,128)(4,1)S(1)} %copy-done.72, pred[128,8,128]{2,1,0:T(8,128)(4,1)S(1)} %get-tuple-element.233, pred[128,8,128]{2,1,0:T(8,128)(4,1)S(1)} %get-tuple-element.232, ...), kind=kLoop, calls=%fused_computation.180 | loop fusion | flops 2097152 | bytes 2621504
  83.5 10.9 %bitcast_dynamic-update-slice_fusion = f32[5,128,8,128]{3,2,1,0:T(8,128)S(1)} fusion(f32[5,128,8,128]{3,2,1,0:T(8,128)S(1)} %bitcast_dynamic-update-slice_fusion.1, pred[128,8,128]{2,1,0:T(8,128)(4,1)S(1)} %copy-done.72, pred[128,8,128]{2,1,0:T(8,128)(4,1)S(1)} %get-tuple-element.233, pred[128,8,128]{2,1,0:T(8,128)(4,1)S(1)} %get-tuple-element.232, ...), kind=kLoop, calls=%fused_computation.179 | loop fusion | flops 2097152 | bytes 2621504 | tf_op jit(solution)/shard_map/stack | solution.py:140
  96.1 3.5 collective-permute-start
  101.3 5.8 fusion.88
  111.8 3.3 copy.102
  115.1 4.5 collective-permute-start.2
  126.8 11.1 %select_maximum_fusion = f32[5,130,10,130]{3,2,1,0:T(8,128)S(1)} fusion(f32[5,128,10,1]{3,2,1,0:T(8,128)} %copy.105, f32[5,128,10,1]{3,2,1,0:T(8,128)} %copy.104, f32[5,128,1,128]{3,2,1,0:T(1,128)S(1)} %collective-permute-done.1, f32[5,128,8,128]{3,2,1,0:T(8,128)} %copy-done.19, f32[5,128,1,128]{3,2,1,0:T(1,128)S(1)} %collective-permute-done), kind=kLoop, calls=%fused_computation.6 | loop fusion | flops 10140000 | bytes 6708000 | tf_op jit(solution)/shard_map/concatenate | solution.py:19
  147.7 13.0 %multiply_reduce_fusion.14 = (f32[]{:T(128)}, f32[128,8,128]{2,1,0:T(8,128)S(1)}, f32[128,8,128]{2,1,0:T(8,128)}) fusion(f32[129,8,128]{2,1,0:T(8,128)S(1)} %get-tuple-element.216, f32[128,8,129]{2,1,0:T(8,128)S(1)} %get-tuple-element.214, f32[128,9,128]{2,1,0:T(8,128)S(1)} %get-tuple-element.212, f32[128,8,128]{2,1,0:T(8,128)S(1)} %get-tuple-element.237, ...), kind=kLoop, calls=%fused_computation.212 | loop fusion | flops 5111807 | bytes 8388676 | tf_op jit(solution)/shard_map/reduce_sum | solution.py:109
  160.7 47.3 %psum.63 = f32[]{:T(128)} all-reduce(f32[]{:T(128)} %get-tuple-element.209), channel_id=1, replica_groups=mesh['gx'=8,'gy'=4] {'gx','gy'}, use_global_device_ids=true, to_apply=%region_3.5 | all-reduce | flops 1 | bytes 8 | tf_op jit(solution)/shard_map/psum | solution.py:109
  220.6 4.5 collective-permute-start.6
  228.0 3.7 fusion.5
  240.8 43.8 %psum.64 = f32[1]{0:T(128)} all-reduce(f32[1]{0:T(128)} %bitcast.111), channel_id=1, replica_groups=mesh['gx'=8,'gy'=4] {'gx','gy'}, use_global_device_ids=true, to_apply=%region_5.7 | all-reduce | flops 1 | bytes 8 | tf_op jit(solution)/shard_map/psum | solution.py:177
  285.9 40.2 %psum.65 = f32[]{:T(128)} all-reduce(f32[]{:T(128)} %multiply_reduce_fusion.12), channel_id=1, replica_groups=mesh['gx'=8,'gy'=4] {'gx','gy'}, use_global_device_ids=true, to_apply=%region_7.9 | all-reduce | flops 1 | bytes 8 | tf_op jit(solution)/shard_map/psum | solution.py:109
  339.3 4.8 collective-permute-start.10
  347.1 3.7 fusion.4
  358.8 43.9 %psum.66 = f32[2]{0:T(128)S(1)} all-reduce(f32[2]{0:T(128)S(1)} %pad_maximum_fusion.29), channel_id=1, replica_groups=mesh['gx'=8,'gy'=4] {'gx','gy'}, use_global_device_ids=true, to_apply=%region_10.12 | all-reduce | flops 2 | bytes 16 | tf_op jit(solution)/shard_map/psum | solution.py:177
  406.5 40.8 %psum.67 = f32[]{:T(128)} all-reduce(f32[]{:T(128)} %get-tuple-element.193), channel_id=1, replica_groups=mesh['gx'=8,'gy'=4] {'gx','gy'}, use_global_device_ids=true, to_apply=%region_12.14 | all-reduce | flops 1 | bytes 8 | tf_op jit(solution)/shard_map/psum | solution.py:109
  459.8 4.9 collective-permute-start.14
  467.6 3.7 fusion.3
  479.5 43.1 %psum.68 = f32[3]{0:T(128)S(1)} all-reduce(f32[3]{0:T(128)S(1)} %pad_maximum_fusion.30), channel_id=1, replica_groups=mesh['gx'=8,'gy'=4] {'gx','gy'}, use_global_device_ids=true, to_apply=%region_17.19 | all-reduce | flops 3 | bytes 24 | tf_op jit(solution)/shard_map/psum | solution.py:177
  523.3 3.5 multiply_reduce_fusion.5
  526.8 41.5 %psum.69 = f32[]{:T(128)} all-reduce(f32[]{:T(128)} %get-tuple-element.188), channel_id=1, replica_groups=mesh['gx'=8,'gy'=4] {'gx','gy'}, use_global_device_ids=true, to_apply=%region_19.21 | all-reduce | flops 1 | bytes 8 | tf_op jit(solution)/shard_map/psum | solution.py:109
  581.8 4.5 collective-permute-start.18
  600.7 3.7 fusion.2
  614.7 42.1 %psum.70 = f32[4]{0:T(128)S(1)} all-reduce(f32[4]{0:T(128)S(1)} %pad_maximum_fusion.31), channel_id=1, replica_groups=mesh['gx'=8,'gy'=4] {'gx','gy'}, use_global_device_ids=true, to_apply=%region_25.27 | all-reduce | flops 4 | bytes 32 | tf_op jit(solution)/shard_map/psum | solution.py:177
  659.4 3.5 multiply_reduce_fusion
  664.3 41.5 %psum.71 = f32[]{:T(128)} all-reduce(f32[]{:T(128)} %multiply_reduce_fusion), channel_id=1, replica_groups=mesh['gx'=8,'gy'=4] {'gx','gy'}, use_global_device_ids=true, to_apply=%region_27.29 | all-reduce | flops 1 | bytes 8 | tf_op jit(solution)/shard_map/psum | solution.py:109
  (325 shorter events, 161.2 us)
Async XLA Ops:
  4.5 21.7 %all-to-all-start = ((f32[32,4,8,128]{3,2,1,0:T(8,128)}), f32[32,4,8,128]{3,2,1,0:T(8,128)S(1)}, u32[]{:S(2)}, u32[]{:S(2)}) async-start(f32[32,4,8,128]{3,2,1,0:T(8,128)} %get-tuple-element.366), calls=%async_computation | async-start | bytes 1048576 | tf_op jit(solution)/shard_map/all_to_all | solution.py:127
  26.2 19.7 %all-to-all-start.1 = ((f32[32,4,8,128]{3,2,1,0:T(8,128)}), f32[32,4,8,128]{3,2,1,0:T(8,128)S(1)}, u32[]{:S(2)}, u32[]{:S(2)}) async-start(f32[32,4,8,128]{3,2,1,0:T(8,128)} %get-tuple-element.365), calls=%async_computation.1 | async-start | bytes 1048576 | tf_op jit(solution)/shard_map/all_to_all | solution.py:128
  44.3 39.1 %copy-start.56 = (pred[128,8,128]{2,1,0:T(8,128)(4,1)}, pred[128,8,128]{2,1,0:T(8,128)(4,1)S(1)}, u32[]{:S(2)}) copy-start(pred[128,8,128]{2,1,0:T(8,128)(4,1)S(1)} %get-tuple-element.226) | copy-start | bytes 393220
  44.3 39.1 %copy-start.58 = (pred[128,8,128]{2,1,0:T(8,128)(4,1)}, pred[128,8,128]{2,1,0:T(8,128)(4,1)S(1)}, u32[]{:S(2)}) copy-start(pred[128,8,128]{2,1,0:T(8,128)(4,1)S(1)} %get-tuple-element.227) | copy-start | bytes 393220
  44.3 39.1 %copy-start.60 = (pred[128,8,128]{2,1,0:T(8,128)(4,1)}, pred[128,8,128]{2,1,0:T(8,128)(4,1)S(1)}, u32[]{:S(2)}) copy-start(pred[128,8,128]{2,1,0:T(8,128)(4,1)S(1)} %get-tuple-element.228) | copy-start | bytes 393220
  44.3 39.1 %copy-start.62 = (pred[128,8,128]{2,1,0:T(8,128)(4,1)}, pred[128,8,128]{2,1,0:T(8,128)(4,1)S(1)}, u32[]{:S(2)}) copy-start(pred[128,8,128]{2,1,0:T(8,128)(4,1)S(1)} %get-tuple-element.229) | copy-start | bytes 393220
  44.4 39.1 %copy-start.64 = (pred[128,8,128]{2,1,0:T(8,128)(4,1)}, pred[128,8,128]{2,1,0:T(8,128)(4,1)S(1)}, u32[]{:S(2)}) copy-start(pred[128,8,128]{2,1,0:T(8,128)(4,1)S(1)} %get-tuple-element.230) | copy-start | bytes 393220
  44.4 39.1 %copy-start.66 = (pred[128,8,128]{2,1,0:T(8,128)(4,1)}, pred[128,8,128]{2,1,0:T(8,128)(4,1)S(1)}, u32[]{:S(2)}) copy-start(pred[128,8,128]{2,1,0:T(8,128)(4,1)S(1)} %get-tuple-element.231) | copy-start | bytes 393220
  44.4 97.5 %copy-start.41 = (f32[128,8,128]{2,1,0:T(8,128)}, f32[128,8,128]{2,1,0:T(8,128)S(1)}, u32[]{:S(2)}) copy-start(f32[128,8,128]{2,1,0:T(8,128)S(1)} %get-tuple-element.218) | copy-start | bytes 1572868
  94.8 4.8 collective-permute-start.1
  96.1 4.3 collective-permute-start
  110.5 9.9 %collective-permute-start.3 = (f32[5,128,10,1]{1,3,2,0:T(1,128)S(1)}, f32[5,128,10,1]{1,3,2,0:T(1,128)S(1)}, u32[]{:S(2)}, u32[]{:S(2)}) collective-permute-start(f32[5,128,10,1]{1,3,2,0:T(1,128)S(1)} %copy.103), channel_id=1, source_target_pairs={{1,0},{2,1},{3,2},{5,4},{6,5},{7,6},{9,8},{10,9},{11,10},{13,12},{... | collective-permute-start | bytes 76808 | tf_op jit(solution)/shard_map/ppermute | solution.py:23
  115.1 8.5 %collective-permute-start.2 = (f32[5,128,10,1]{1,3,2,0:T(1,128)S(1)}, f32[5,128,10,1]{1,3,2,0:T(1,128)S(1)}, u32[]{:S(2)}, u32[]{:S(2)}) collective-permute-start(f32[5,128,10,1]{1,3,2,0:T(1,128)S(1)} %copy.102), channel_id=1, source_target_pairs={{0,1},{1,2},{2,3},{4,5},{5,6},{6,7},{8,9},{9,10},{10,11},{12,13},{... | collective-permute-start | bytes 76808 | tf_op jit(solution)/shard_map/ppermute | solution.py:21
  142.6 89.2 %copy-start.20 = (f32[129,8,128]{2,1,0:T(8,128)}, f32[129,8,128]{2,1,0:T(8,128)S(1)}, u32[]{:S(2)}) copy-start(f32[129,8,128]{2,1,0:T(8,128)S(1)} %get-tuple-element.217) | copy-start | bytes 1585156
  208.8 4.3 collective-permute-start.4
  210.1 3.9 collective-permute-start.5
  217.5 7.6 %collective-permute-start.7 = (f32[128,10,1]{0,1,2:T(8,128)S(1)}, f32[128,10,1]{0,1,2:T(8,128)S(1)}, u32[]{:S(2)}, u32[]{:S(2)}) collective-permute-start(f32[128,10,1]{0,1,2:T(8,128)S(1)} %copy.107), channel_id=1, source_target_pairs={{1,0},{2,1},{3,2},{5,4},{6,5},{7,6},{9,8},{10,9},{11,10},{13,12},{... | collective-permute-start | bytes 15368 | tf_op jit(solution)/shard_map/ppermute | solution.py:23
  220.6 6.0 collective-permute-start.6
  240.8 114.1 %copy-start.36 = (f32[128,8,128]{2,1,0:T(8,128)}, f32[128,8,128]{2,1,0:T(8,128)S(1)}, u32[]{:S(2)}) copy-start(f32[128,8,128]{2,1,0:T(8,128)S(1)} %get-tuple-element.200) | copy-start | bytes 1572868
  327.6 4.3 collective-permute-start.8
  328.9 3.9 collective-permute-start.9
  336.4 7.8 %collective-permute-start.11 = (f32[128,10,1]{0,1,2:T(8,128)S(1)}, f32[128,10,1]{0,1,2:T(8,128)S(1)}, u32[]{:S(2)}, u32[]{:S(2)}) collective-permute-start(f32[128,10,1]{0,1,2:T(8,128)S(1)} %copy.113), channel_id=1, source_target_pairs={{1,0},{2,1},{3,2},{5,4},{6,5},{7,6},{9,8},{10,9},{11,10},{13,12},{... | collective-permute-start | bytes 15368 | tf_op jit(solution)/shard_map/ppermute | solution.py:23
  339.3 6.3 collective-permute-start.10
  448.1 5.0 collective-permute-start.12
  449.4 3.9 collective-permute-start.13
  456.8 7.9 %collective-permute-start.15 = (f32[128,10,1]{0,1,2:T(8,128)S(1)}, f32[128,10,1]{0,1,2:T(8,128)S(1)}, u32[]{:S(2)}, u32[]{:S(2)}) collective-permute-start(f32[128,10,1]{0,1,2:T(8,128)S(1)} %copy.119), channel_id=1, source_target_pairs={{1,0},{2,1},{3,2},{5,4},{6,5},{7,6},{9,8},{10,9},{11,10},{13,12},{... | collective-permute-start | bytes 15368 | tf_op jit(solution)/shard_map/ppermute | solution.py:23
  459.8 6.4 collective-permute-start.14
  570.2 4.4 collective-permute-start.16
  571.5 3.9 collective-permute-start.17
  578.9 18.9 %collective-permute-start.19 = (f32[128,10,1]{0,1,2:T(8,128)S(1)}, f32[128,10,1]{0,1,2:T(8,128)S(1)}, u32[]{:S(2)}, u32[]{:S(2)}) collective-permute-start(f32[128,10,1]{0,1,2:T(8,128)S(1)} %copy.125), channel_id=1, source_target_pairs={{1,0},{2,1},{3,2},{5,4},{6,5},{7,6},{9,8},{10,9},{11,10},{13,12},{... | collective-permute-start | bytes 15368 | tf_op jit(solution)/shard_map/ppermute | solution.py:23
  581.8 17.5 %collective-permute-start.18 = (f32[128,10,1]{0,1,2:T(8,128)S(1)}, f32[128,10,1]{0,1,2:T(8,128)S(1)}, u32[]{:S(2)}, u32[]{:S(2)}) collective-permute-start(f32[128,10,1]{0,1,2:T(8,128)S(1)} %copy.124), channel_id=1, source_target_pairs={{0,1},{1,2},{2,3},{4,5},{5,6},{6,7},{8,9},{9,10},{10,11},{12,13},{... | collective-permute-start | bytes 15368 | tf_op jit(solution)/shard_map/ppermute | solution.py:21
  659.4 75.8 %copy-start.1 = (f32[128,8,128]{2,1,0:T(8,128)S(1)}, f32[128,8,128]{2,1,0:T(8,128)}, u32[]{:S(2)}) copy-start(f32[128,8,128]{2,1,0:T(8,128)} %param.39) | copy-start | bytes 1572868
  (72 other events, 454.9 us)
where the time goes:
time: 746 us; the launch traced here: 735 us
  blocking collectives  384 us (51%)
  other arithmetic  147 us (20%)
  local copies, waits for them, and re-layouts  96.7 us (13%)
  starting transfers between devices  63.4 us (8%)
  between operations  28.8 us (4%)
  waiting for transfers between devices  15.1 us (2%)
    psum x5, blocking collectives, global_length(): return jnp.sqrt(lax.psum(jnp.sum(field * field), ('gx', 'gy')))  211 us
    psum x4, blocking collectives, body(): summed = lax.psum(local_products, ('gx', 'gy'))  173 us
    ppermute x10, starting transfers between devices, extended(): lax.ppermute(tail, axis, [(i, (i + 1) % count) for i in range(ends)])  39 us
    reduce_sum x5, other arithmetic, global_length(): return jnp.sqrt(lax.psum(jnp.sum(field * field), ('gx', 'gy')))  24.5 us
    slice x15, local copies, waits for them, and re-layouts, extended(): lax.slice_in_dim(cells, cells.shape[dim] - width, cells.shape[dim], axis=...  23.2 us
    mul x1, other arithmetic, retention(): saturation = jnp.exp(exponent * jnp.log(inverse))  21.3 us
  transfers between devices with their start and end apart: 22, of which 6 were waited for; matrix products, arithmetic and copies ran while one was open for 7% of the time, Pallas kernels for 0%

commit v1 on v0

v1 whole, which is shorter than its diff:
```python
import functools

import jax
import jax.numpy as jnp
from jax import lax
from jax.experimental import pallas as pl
from jax.experimental.pallas import tpu as pltpu
from jax.sharding import PartitionSpec as P

MATERIALS = 16
ITERS = 4
STORE = 4.0
MESH = pl.DeviceIdType.MESH
TILE = 8


def expm1_negative(t):
    series = 1.0 + t * (1.0 / 8.0)
    for k in (7.0, 6.0, 5.0, 4.0, 3.0, 2.0):
        series = 1.0 + t * (1.0 / k) * series
    return jnp.where(t > -0.4, t * series, jnp.exp(t) - 1.0)


def saturation_parts(level, alpha_cell, expo_cell):
    scaled = alpha_cell * -level
    power = jnp.exp(expo_cell * jnp.log(scaled))
    exponent = 1.0 - 1.0 / expo_cell
    inverse = 1.0 / (1.0 + power)
    return power, exponent, inverse, exponent * jnp.log(inverse)


def rotate(column, rotations):
    column = list(column)
    for i, (cosine, sine) in enumerate(rotations):
        top, low = column[i], column[i + 1]
        column[i] = cosine * top + sine * low
        column[i + 1] = cosine * low - sine * top
    return column


def kernel(
    n_gx,
    n_gy,
    slab,
    order_ref,
    cond_ref,
    alpha_ref,
    expo_ref,
    cap_ref,
    head_ref,
    old_ref,
    ids_ref,
    out_ref,
    packed,
    arrived,
    zorder,
    level,
    cond_x,
    cond_y,
    cond_z,
    alpha_f,
    expo_f,
    cap_f,
    trans,
    store_f,
    diag_f,
    coef,
    krylov,
    basis,
    rim_c_out,
    rim_c,
    rim_h_out,
    rim_h,
    rim_v_out,
    rim_v,
    red_out,
    red_in,
    a2a_send,
    a2a_recv,
    rim_send,
    rim_recv,
    red_send,
    red_recv,
):
    n = n_gx * n_gy
    nz = ids_ref.shape[0] // TILE
    ny = ids_ref.shape[1]
    gx, gy = lax.axis_index("gx"), lax.axis_index("gy")
    me = gx * n_gy + gy
    block = slab * TILE

    def coords(d):
        return (d // n_gy, d % n_gy)

    zero_tile = jnp.zeros((TILE, nz), jnp.float32)
    zero_face = jnp.zeros((ny, nz), jnp.float32)

    def y_edges(ref, index):
        ref[index + (pl.ds(0, TILE), slice(None))] = zero_tile
        ref[index + (pl.ds((ny + 1) * TILE, TILE), slice(None))] = zero_tile

    y_edges(cond_y, ())
    for f in range(3):
        y_edges(level, (f,))
    for k in range(ITERS):
        y_edges(krylov, (k,))
    for side in range(2):
        rim_c[side] = zero_face
        for f in range(3):
            rim_h[side, f] = zero_face
        for k in range(ITERS):
            rim_v[k, side] = zero_face

    barrier = pltpu.get_barrier_semaphore()

    def greet(t, carry):
        pl.semaphore_signal(
            barrier, inc=1, device_id=coords(lax.rem(me + t, n)), device_id_type=MESH
        )
        return carry

    lax.fori_loop(1, n, greet, 0)

    def pack(d, carry):
        source = order_ref[0, d]
        packed[d, pl.ds(0, block), :] = head_ref[source]
        packed[d, pl.ds(block, block), :] = old_ref[source]
        return carry

    lax.fori_loop(0, n, pack, 0)
    pl.semaphore_wait(barrier, n - 1)

    def send_block(t, carry):
        d = lax.rem(me + t, n)
        pltpu.make_async_remote_copy(
            packed.at[d], arrived.at[me], a2a_send, a2a_recv, device_id=coords(d), device_id_type=MESH
        ).start()
        return carry

    lax.fori_loop(1, n, send_block, 0)
    arrived[me] = packed[me]

    wanted = (gx > 0, gx < n_gx - 1, gy > 0, gy < n_gy - 1)
    opposite = (wanted[1], wanted[0], wanted[3], wanted[2])
    partner = ((gx - 1, gy), (gx + 1, gy), (gx, gy - 1), (gx, gy + 1))

    def rim_copies(slot, x_out, x_in, y_ref):
        first, last = pl.ds(TILE, TILE), pl.ds(ny * TILE, TILE)
        below, above = pl.ds(0, TILE), pl.ds((ny + 1) * TILE, TILE)
        ends = (
            (x_out.at[0], x_in.at[1]),
            (x_out.at[1], x_in.at[0]),
            (y_ref(first), y_ref(above)),
            (y_ref(last), y_ref(below)),
        )
        return [
            pltpu.make_async_remote_copy(
                source,
                target,
                rim_send.at[slot, i],
                rim_recv.at[slot, i],
                device_id=partner[i],
                device_id_type=MESH,
            )
            for i, (source, target) in enumerate(ends)
        ]

    def start(copies):
        for copy, go in zip(copies, wanted):
            pl.when(go)(copy.start)

    def finish_recv(copies):
        for copy, go in zip(copies, opposite):
            pl.when(go)(copy.wait_recv)

    def finish_send(copies):
        for copy, go in zip(copies, wanted):
            pl.when(go)(copy.wait_send)

    rows = 4
    chunk = rows * TILE

    def cells(ref, i, index=(), offset=0):
        at = pl.ds(pl.multiple_of(i * chunk + offset, TILE), chunk)
        return ref[index + (at, slice(None))].reshape(rows, TILE, nz)

    def put(ref, i, value, index=(), offset=0):
        at = pl.ds(pl.multiple_of(i * chunk + offset, TILE), chunk)
        ref[index + (at, slice(None))] = value.reshape(chunk, nz)

    chunks = ny // rows

    for x in range(TILE):
        ids = ids_ref[pl.ds(x, nz, stride=TILE), :].T
        kinds = [jnp.zeros(ids.shape, jnp.float32) for i in range(6)]
        for m in range(MATERIALS):
            match = ids == m
            values = (
                cond_ref[0, m],
                cond_ref[1, m],
                cond_ref[2, m],
                alpha_ref[m],
                expo_ref[m],
                cap_ref[m],
            )
            kinds = [jnp.where(match, value, kind) for value, kind in zip(values, kinds)]
        here = pl.ds(x, ny, stride=TILE)
        cond_x[here, :] = kinds[0]
        cond_y[pl.ds(TILE + x, ny, stride=TILE), :] = kinds[1]
        cond_z[here, :] = kinds[2]
        alpha_f[here, :] = kinds[3]
        expo_f[here, :] = kinds[4]
        cap_f[here, :] = kinds[5]

    rim_c_out[0] = cond_x[pl.ds(0, ny, stride=TILE), :]
    rim_c_out[1] = cond_x[pl.ds(TILE - 1, ny, stride=TILE), :]
    cond_copies = rim_copies(0, rim_c_out, rim_c, lambda at: cond_y.at[at])
    start(cond_copies)
    finish_recv(cond_copies)

    shape = (rows, TILE, nz)
    x_at = lax.broadcasted_iota(jnp.int32, shape, 1)
    z_at = lax.broadcasted_iota(jnp.int32, shape, 2)

    def rim_rows(ref, i, index):
        at = pl.ds(i * rows, rows)
        return jnp.broadcast_to(ref[index + (at, slice(None))].reshape(rows, 1, nz), shape)

    def x_pair(v, low_rim, high_rim):
        low = jnp.where(x_at == 0, low_rim, pltpu.roll(v, 1, 1))
        high = jnp.where(x_at == TILE - 1, high_rim, pltpu.roll(v, TILE - 1, 1))
        return low, high

    def z_pair(v):
        return pltpu.roll(v, 1, 2), pltpu.roll(v, nz - 1, 2)

    def mean(a, b):
        return 2.0 * a * b / (a + b)

    def transmissibility(i, carry):
        kx = cells(cond_x, i)
        low, high = x_pair(kx, rim_rows(rim_c, i, (0,)), rim_rows(rim_c, i, (1,)))
        put(trans, i, mean(low, kx), (0,))
        put(trans, i, mean(kx, high), (1,))
        ky = cells(cond_y, i, (), TILE)
        put(trans, i, mean(cells(cond_y, i), ky), (2,))
        put(trans, i, mean(ky, cells(cond_y, i, (), 2 * TILE)), (3,))
        kz = cells(cond_z, i)
        low, high = z_pair(kz)
        put(trans, i, jnp.where(z_at == 0, 0.0, mean(low, kz)), (4,))
        put(trans, i, jnp.where(z_at == nz - 1, 0.0, mean(kz, high)), (5,))
        return carry

    lax.fori_loop(0, chunks, transmissibility, 0)

    others = pl.ds(0, n - 1)
    arrival = pltpu.make_async_remote_copy(
        packed.at[others], arrived.at[others], a2a_send, a2a_recv, device_id=coords(lax.rem(me + 1, n)), device_id_type=MESH
    )
    arrival.wait_recv()

    def unpack(p, carry):
        source = order_ref[1, p]
        at = pl.ds(pl.multiple_of(p * block, TILE), block)
        both = arrived[source]
        zorder[0, at, :] = both[:block]
        zorder[1, at, :] = both[block:]
        return carry

    lax.fori_loop(0, n, unpack, 0)
    for x in range(TILE):
        level[0, pl.ds(TILE + x, ny, stride=TILE), :] = zorder[0, pl.ds(x, nz, stride=TILE), :].T
        store_f[pl.ds(x, ny, stride=TILE), :] = zorder[1, pl.ds(x, nz, stride=TILE), :].T

    def retention(i, carry):
        alpha_cell, expo_cell = cells(alpha_f, i), cells(expo_f, i)
        capacity = STORE * cells(cap_f, i)
        head = cells(level, i, (0,), TILE)
        power, exponent, inverse, log_sat = saturation_parts(head, alpha_cell, expo_cell)
        rest = power * inverse
        root = jnp.exp(0.5 * log_sat)
        saturation = root * root
        inner = -expm1_negative(exponent * jnp.log1p(-inverse))
        gain = (expo_cell - 1.0) / -head
        put(level, i, root * inner * inner, (1,), TILE)
        put(level, i, root * inner * gain * (0.5 * rest * inner + 2.0 * (1.0 - inner) * inverse), (2,), TILE)
        old = saturation_parts(cells(store_f, i), alpha_cell, expo_cell)
        put(store_f, i, capacity * (saturation - jnp.exp(old[3])))
        put(diag_f, i, capacity * saturation * rest * gain)
        return carry

    lax.fori_loop(0, chunks, retention, 0)
    for f in range(3):
        rim_h_out[0, f] = level[f, pl.ds(TILE, ny, stride=TILE), :]
        rim_h_out[1, f] = level[f, pl.ds(2 * TILE - 1, ny, stride=TILE), :]
    level_copies = rim_copies(1, rim_h_out, rim_h, lambda at: level.at[:, at])
    start(level_copies)
    finish_recv(level_copies)

    def assemble(i, carry):
        here = [cells(level, i, (f,), TILE) for f in range(3)]
        pairs = []
        sides = [
            x_pair(here[f], rim_rows(rim_h, i, (0, f)), rim_rows(rim_h, i, (1, f))) for f in range(3)
        ]
        pairs += [[s[0] for s in sides], [s[1] for s in sides]]
        pairs += [[cells(level, i, (f,), 2 * TILE * side) for f in range(3)] for side in range(2)]
        sides = [z_pair(here[f]) for f in range(3)]
        pairs += [[s[0] for s in sides], [s[1] for s in sides]]
        head, rel, drel = here
        total = -cells(store_f, i)
        centre = cells(diag_f, i)
        for face, (head_b, rel_b, drel_b) in enumerate(pairs):
            half = 0.5 * cells(trans, i, (face,))
            rise = 1.0 if face >= 4 else 0.0
            along = half * (rel + rel_b)
            if face % 2:
                potential = head_b - head + rise
                slope = half * potential
                total = total + along * potential
                centre = centre + along - slope * drel
                put(coef, i, -along - slope * drel_b, (1 + face,))
            else:
                potential = head - head_b + rise
                slope = half * potential
                total = total - along * potential
                centre = centre + along + slope * drel
                put(coef, i, slope * drel_b - along, (1 + face,))
        put(coef, i, centre, (0,))
        put(krylov, i, total, (0,), TILE)
        return carry

    lax.fori_loop(0, chunks, assemble, 0)

    def send_rims(k):
        rim_v_out[k, 0] = krylov[k, pl.ds(TILE, ny, stride=TILE), :]
        rim_v_out[k, 1] = krylov[k, pl.ds(2 * TILE - 1, ny, stride=TILE), :]
        copies = rim_copies(2 + k, rim_v_out.at[k], rim_v.at[k], lambda at: krylov.at[k, at])
        start(copies)
        return copies

    def fold(value):
        return jnp.sum(value, axis=0)

    none = jnp.zeros((TILE, nz), jnp.float32)

    def apply_stencil(k, i):
        v = cells(krylov, i, (k,), TILE)
        x_low, x_high = x_pair(v, rim_rows(rim_v, i, (k, 0)), rim_rows(rim_v, i, (k, 1)))
        z_low, z_high = z_pair(v)
        total = cells(coef, i, (0,)) * v
        total = total + cells(coef, i, (1,)) * x_low + cells(coef, i, (2,)) * x_high
        total = total + cells(coef, i, (3,)) * cells(krylov, i, (k,))
        total = total + cells(coef, i, (4,)) * cells(krylov, i, (k,), 2 * TILE)
        total = total + cells(coef, i, (5,)) * z_low + cells(coef, i, (6,)) * z_high
        return v, total

    row_at = lax.broadcasted_iota(jnp.int32, (TILE, nz), 0)

    def send_sums(k, sums):
        local = none
        for r, value in enumerate(sums):
            local = jnp.where(row_at == r, jnp.sum(value, axis=0, keepdims=True), local)
        red_out[k] = local
        red_in[k, me] = local

        def one(t, carry):
            d = lax.rem(me + t, n)
            pltpu.make_async_remote_copy(
                red_out.at[k],
                red_in.at[k, me],
                red_send.at[k],
                red_recv.at[k],
                device_id=coords(d),
                device_id_type=MESH,
            ).start()
            return carry

        lax.fori_loop(1, n, one, 0)

    def sum_copy(k):
        return pltpu.make_async_remote_copy(
            red_in.at[k, others],
            red_in.at[k, others],
            red_send.at[k],
            red_recv.at[k],
            device_id=coords(lax.rem(me + 1, n)),
            device_id_type=MESH,
        )

    def take_sums(k, count):
        sum_copy(k).wait_recv()
        total = jnp.sum(jnp.sum(red_in[k], axis=0), axis=1, keepdims=True)
        return [jnp.broadcast_to(total[r : r + 1, :], (TILE, nz)) for r in range(count)]

    rim_sets = [send_rims(0)]
    finish_recv(rim_sets[0])

    def first(i, sums):
        v, image = apply_stencil(0, i)
        put(krylov, i, image, (1,), TILE)
        return (sums[0] + fold(v * v), sums[1] + fold(image * v), sums[2] + fold(image * image))

    sums = lax.fori_loop(0, chunks, first, (none, none, none))
    rotations, columns, target = [], [], None
    for j in range(ITERS):
        if j + 1 < ITERS:
            rim_sets.append(send_rims(j + 1))
        send_sums(j, sums)
        if j + 1 < ITERS:
            finish_recv(rim_sets[j + 1])

            def ahead(i, carry):
                put(basis, i, apply_stencil(j + 1, i)[1], (ITERS,))
                return carry

            lax.fori_loop(0, chunks, ahead, 0)
        got = take_sums(j, j + 2 if j else 3)
        if j == 0:
            square = got[0]
            beta = jnp.sqrt(square)
            shrink = 1.0 / beta
            products = [got[1] / square]
            own_square = got[2] / square
            target = [beta] + [none] * ITERS
        else:
            products, own_square = got[: j + 1], got[j + 1]
        rest = own_square
        for value in products:
            rest = rest - value * value
        length = jnp.sqrt(rest)
        column = rotate(products + [length], rotations)
        radius = jnp.sqrt(column[j] * column[j] + column[j + 1] * column[j + 1])
        turn = (column[j] / radius, column[j + 1] / radius)
        column[j] = radius
        rotations.append(turn)
        columns.append(column)
        target[j], target[j + 1] = turn[0] * target[j], -turn[1] * target[j]
        if j + 1 == ITERS:
            break
        inverse_length = 1.0 / length
        if j == 0:
            finish_send(rim_sets[0])

        def advance(i, sums):
            if j == 0:
                low = cells(krylov, i, (0,), TILE) * shrink
                put(basis, i, low, (0,))
                lows = [low]
                images = [cells(krylov, i, (1,), TILE) * shrink]
                put(krylov, i, images[0], (0,), TILE)
                further = cells(basis, i, (ITERS,)) * shrink
            else:
                lows = [cells(basis, i, (k,)) for k in range(j + 1)]
                slots = [0] + list(range(2, j + 2))
                images = [cells(krylov, i, (slot,), TILE) for slot in slots]
                further = cells(basis, i, (ITERS,))
            fresh = images[-1]
            for value, low, image in zip(products, lows, images):
                fresh = fresh - value * low
                further = further - value * image
            fresh = fresh * inverse_length
            further = further * inverse_length
            put(basis, i, fresh, (j + 1,))
            put(krylov, i, further, (j + 2,), TILE)
            lows.append(fresh)
            return tuple(
                s + fold(further * other) for s, other in zip(sums, lows + [further])
            )

        sums = lax.fori_loop(0, chunks, advance, (none,) * (j + 3))

    coeffs = [None] * ITERS
    for j in reversed(range(ITERS)):
        running = target[j]
        for k in range(j + 1, ITERS):
            running = running - columns[k][j] * coeffs[k]
        coeffs[j] = running / columns[j][j]

    def combine(i, carry):
        total = coeffs[0] * cells(basis, i, (0,))
        for k in range(1, ITERS):
            total = total + coeffs[k] * cells(basis, i, (k,))
        put(diag_f, i, total)
        return carry

    lax.fori_loop(0, chunks, combine, 0)
    for x in range(TILE):
        out_ref[pl.ds(x, nz, stride=TILE), :] = diag_f[pl.ds(x, ny, stride=TILE), :].T

    arrival.wait_send()
    finish_send(cond_copies)
    finish_send(level_copies)
    for copies in rim_sets[1:]:
        finish_send(copies)
    for k in range(ITERS):
        sum_copy(k).wait_send()


def body(held_head, held_head_old, material_ids, block_map, conductivity, vg_alpha, vg_n, capacity):
    n_gx, n_gy = lax.axis_size("gx"), lax.axis_size("gy")
    devices = n_gx * n_gy
    own_index = lax.axis_index(("gx", "gy"))
    layers, width, depth = held_head.shape
    slab = layers // devices
    numbers = jnp.arange(devices, dtype=jnp.int32)
    own_row = block_map[own_index]
    send_order = jnp.sum(
        jnp.where(own_row[None, :] == numbers[:, None], numbers[None, :], 0), axis=1
    )
    source_of = jnp.sum(jnp.where(block_map == own_index, numbers[:, None], 0), axis=0)
    order = jnp.stack([send_order, source_of])
    count = layers * width
    padded = (depth + 2) * width
    f32 = jnp.float32
    vmem = pltpu.VMEM
    smem_spec = pl.BlockSpec(memory_space=pltpu.SMEM)
    vmem_spec = pl.BlockSpec(memory_space=pltpu.VMEM)
    plain = vmem((depth * width, layers), f32)
    flat = (count, depth)
    update = pl.pallas_call(
        functools.partial(kernel, n_gx, n_gy, slab),
        out_shape=jax.ShapeDtypeStruct(flat, f32),
        in_specs=[smem_spec] * 5 + [vmem_spec] * 3,
        out_specs=vmem_spec,
        scratch_shapes=[
            vmem((devices, 2 * slab * width, depth), f32),
            vmem((devices, 2 * slab * width, depth), f32),
            vmem((2, count, depth), f32),
            vmem((3, padded, layers), f32),
            plain,
            vmem((padded, layers), f32),
            plain,
            plain,
            plain,
            plain,
            vmem((6, depth * width, layers), f32),
            plain,
            plain,
            vmem((7, depth * width, layers), f32),
            vmem((ITERS + 1, padded, layers), f32),
            vmem((ITERS + 1, depth * width, layers), f32),
            vmem((2, depth, layers), f32),
            vmem((2, depth, layers), f32),
            vmem((2, 3, depth, layers), f32),
            vmem((2, 3, depth, layers), f32),
            vmem((ITERS, 2, depth, layers), f32),
            vmem((ITERS, 2, depth, layers), f32),
            vmem((ITERS, width, layers), f32),
            vmem((ITERS, devices, width, layers), f32),
            pltpu.SemaphoreType.DMA,
            pltpu.SemaphoreType.DMA,
            pltpu.SemaphoreType.DMA((ITERS + 2, 4)),
            pltpu.SemaphoreType.DMA((ITERS + 2, 4)),
            pltpu.SemaphoreType.DMA((ITERS,)),
            pltpu.SemaphoreType.DMA((ITERS,)),
        ],
        compiler_params=pltpu.CompilerParams(
            collective_id=0, has_side_effects=True, vmem_limit_bytes=48 * 1024 * 1024
        ),
    )(
        order,
        conductivity,
        vg_alpha,
        vg_n,
        capacity,
        held_head.reshape(devices, slab * width, depth),
        held_head_old.reshape(devices, slab * width, depth),
        material_ids.reshape(flat),
    )
    return update.reshape(layers, width, depth)


def solution(mesh):
    return jax.shard_map(
        body,
        mesh=mesh,
        in_specs=(
            P(("gx", "gy"), None, None),
            P(("gx", "gy"), None, None),
            P(None, "gx", "gy"),
            P(),
            P(),
            P(),
            P(),
            P(),
        ),
        out_specs=P(None, "gx", "gy"),
        check_vma=False,
    )
```

time: 746 us -> 84.4 us (0.11); the launches traced: 735 us -> 84 us
  blocking collectives: 384 us -> 0 us
  other arithmetic: 147 us -> 0.15 us
  local copies, waits for them, and re-layouts: 96.7 us -> 5.32 us
  Pallas kernels: 0 us -> 78.5 us
  starting transfers between devices: 63.4 us -> 0 us
  between operations: 28.8 us -> 0.05 us
  waiting for transfers between devices: 15.1 us -> 0 us
    psum x9 -> x0, blocking collectives: 384 us -> none  [the longest x5 211 us: global_length(): return jnp.sqrt(lax.psum(jnp.sum(field * field), ('gx', 'gy')))]
    pallas_call x0 -> x1, Pallas kernels: none -> 78.5 us  [body(): pl.pallas_call(functools.partial(kernel, n_gx, n_gy, slab), out_shape=jax...]
    ppermute x20 -> x0, starting transfers between devices: 52.1 us -> none  [the longest x10 39 us: extended(): lax.ppermute(tail, axis, [(i, (i + 1) % count) for i in range(ends)])]
    slice x37 -> x0, local copies, waits for them, and re-layouts: 44.3 us -> none  [the longest x15 23.2 us: extended(): lax.slice_in_dim(cells, cells.shape[dim] - width, cells.shape[dim], axis=...]
    mul x9 -> x0, other arithmetic: 40.8 us -> none  [the longest x1 21.3 us: retention(): saturation = jnp.exp(exponent * jnp.log(inverse))]
    reduce_sum x9 -> x0, other arithmetic: 29.6 us -> none  [the longest x5 24.5 us: global_length(): return jnp.sqrt(lax.psum(jnp.sum(field * field), ('gx', 'gy')))]
    ppermute x10 -> x0, local copies, waits for them, and re-layouts: 17.9 us -> none  [the longest x5 9.09 us: extended(): lax.ppermute(head, axis, [((i + 1) % count, i) for i in range(ends)])]
    another operation x7 -> x1, other arithmetic: 17.5 us -> 0.01 us  [body(): order = jnp.stack([send_order, source_of])]
  transfers between devices with their start and end apart: 22 -> 0, of which waited for: 6 -> 0; matrix products, arithmetic and copies ran while one was open for 7% -> 0% of each run, Pallas kernels for 0% -> 0%
where the time goes in v1:
time: 84.4 us; the launch traced here: 84 us
  Pallas kernels  78.5 us (93%)
  local copies, waits for them, and re-layouts  5.32 us (6%)
    pallas_call x1, Pallas kernels, body(): pl.pallas_call(functools.partial(kernel, n_gx, n_gy, slab), out_shape=jax...  78.5 us
    unnamed x17, local copies, waits for them, and re-layouts  5.31 us

profile of v1, /device:TPU:0, one launch (start us, length us, event | category | flops | bytes accessed | tf_op | source)
XLA Modules:
  0.0 84.0 jit_solution(16944407635102174647)
XLA Ops:
  0.0 0.0 copy-start.7
  0.0 0.7 copy-done.7
  0.8 0.1 select_reduce_fusion.1
  0.9 0.0 copy-start.3
  0.9 0.0 copy-start.4
  0.9 0.0 copy-start.5
  0.9 0.0 copy-start.6
  0.9 0.6 copy-done.3
  1.6 0.0 copy-done.4
  1.6 0.0 copy-done.5
  1.6 0.0 copy-done.6
  1.6 0.0 copy-start
  1.6 1.0 %copy-done = f32[128,8,128]{2,1,0:T(8,128)S(1)} copy-done((f32[128,8,128]{2,1,0:T(8,128)S(1)}, f32[128,8,128]{2,1,0:T(8,128)}, u32[]{:S(2)}) %copy-start) | copy-done | bytes 524312
  2.6 0.0 copy-start.1
  2.6 1.0 %copy-done.1 = f32[128,8,128]{2,1,0:T(8,128)S(1)} copy-done((f32[128,8,128]{2,1,0:T(8,128)S(1)}, f32[128,8,128]{2,1,0:T(8,128)}, u32[]{:S(2)}) %copy-start.1) | copy-done | bytes 524312
  3.7 0.0 copy-start.2
  3.7 1.0 %copy-done.2 = s32[128,8,128]{2,1,0:T(8,128)S(1)} copy-done((s32[128,8,128]{2,1,0:T(8,128)S(1)}, s32[128,8,128]{2,1,0:T(8,128)}, u32[]{:S(2)}) %copy-start.2) | copy-done | bytes 524312
  4.7 78.5 %shard_map.82 = f32[1024,128]{1,0:T(8,128)S(1)} custom-call(s32[2,32]{1,0:T(2,128)S(1)} %pad_add_fusion.order_ref, f32[3,16]{1,0:T(4,128)S(1)} %copy-done.3, f32[16]{0:T(128)S(1)} %copy-done.4, f32[16]{0:T(128)S(1)} %copy-done.5, f32[16]{0:T(128)S(1)} %copy-done.6, f32[32,32,128]{2,1,0:T(8,128)S(1)} %bitcast.9, f32[32,32,128]{2,1,0:T(8,128)S(1)} %bitcast.10, ...), custom_call_target="tpu_custom_call" | custom-call | tf_op jit(solution)/shard_map/pallas_call | solution.py:521
  83.3 0.8 copy.10
  (3 shorter events, 0.0 us)
Async XLA Ops:
  0.0 0.7 copy-start.7
  0.9 0.7 copy-start.3
  0.9 0.7 copy-start.4
  0.9 0.7 copy-start.5
  0.9 0.7 copy-start.6
  1.6 1.0 %copy-start = (f32[128,8,128]{2,1,0:T(8,128)S(1)}, f32[128,8,128]{2,1,0:T(8,128)}, u32[]{:S(2)}) copy-start(f32[128,8,128]{2,1,0:T(8,128)} %param.8) | copy-start | bytes 1572868
  2.6 1.0 %copy-start.1 = (f32[128,8,128]{2,1,0:T(8,128)S(1)}, f32[128,8,128]{2,1,0:T(8,128)}, u32[]{:S(2)}) copy-start(f32[128,8,128]{2,1,0:T(8,128)} %param.9) | copy-start | bytes 1572868
  3.7 1.0 %copy-start.2 = (s32[128,8,128]{2,1,0:T(8,128)S(1)}, s32[128,8,128]{2,1,0:T(8,128)}, u32[]{:S(2)}) copy-start(s32[128,8,128]{2,1,0:T(8,128)} %param.10) | copy-start | bytes 1572868
